TPU v7x, 128 devices: a whole 4x4x4 slice. The times are simulated.
128 devices in a mesh: ex: 16 (over x_hi, z, core), lay: 8 (over y, x_lo).
Axes of the slice: x: 4 (x_hi: 2, x_lo: 2; x = x_hi * 2 + x_lo), y: 4, z: 4, core: 2. Of those that a mesh axis runs over, the one named last changes fastest.
Arguments:
- training_gradient_rows: bfloat16 [8192, 16, 4096], P('ex', 'lay'), may hold values from -0.08984375 to 0.08984375
- test_grads: bfloat16 [2048, 16, 4096], P('ex', 'lay'), may hold values from -6 to 6
- inv_out: float32 [16, 64, 64], P('lay'), may hold values from -0.75 to 0.75
- inv_in: float32 [16, 64, 64], P('lay'), may hold values from -0.75 to 0.75
Outputs:
- scores: float32 [2048, 8192], P('lay', 'ex')
All inputs are finite; a program needn't handle non-finite values.
Results may differ from a plain program's by a relative error of at most 0.015.
Values may be sent and summed in bfloat16 or wider, within the bound.
A program may use at most 128 MiB of HBM per device.

v0:
```python
import jax
import jax.numpy as jnp
from jax import lax
from jax.sharding import PartitionSpec as P


def shifted(value, axis, steps):
    count = lax.axis_size(axis)
    pairs = [(source, (source + steps) % count) for source in range(count)]
    return lax.ppermute(value, axis, pairs)


def tile_scoring(block_slab, training_gradient_rows):
    partition_count = jnp.einsum(
        "aec,jec->eaj", block_slab, training_gradient_rows, preferred_element_type=jnp.float32
    )
    rounded = lax.optimization_barrier(partition_count.astype(jnp.bfloat16))
    return jnp.sum(rounded.astype(jnp.float32), axis=0)


def place_tile(table, tile, row_start):
    return lax.dynamic_update_slice(table, tile, (row_start, jnp.zeros((), jnp.int32)))


def body(training_gradient_rows, test_grads, inv_out, inv_in):
    highest = lax.Precision.HIGHEST
    block_rows = test_grads.shape[0]
    layer_count = test_grads.shape[1]
    width = inv_out.shape[1]
    matrix_stack = test_grads.astype(jnp.float32).reshape(block_rows, layer_count, width, width)
    left = jnp.einsum("lab,tlbc->tlac", inv_out, matrix_stack, precision=highest)
    right = jnp.einsum("tlac,lcd->tlad", left, inv_in, precision=highest)
    precond = right.reshape(block_rows, layer_count, width * width).astype(jnp.bfloat16)
    cycle_size = lax.axis_size("ex")
    position = lax.axis_index("ex")
    empty = jnp.zeros((block_rows * cycle_size, training_gradient_rows.shape[0]), jnp.float32)
    group_len = min(8, cycle_size, max(1, 512 // block_rows))
    while cycle_size % group_len != 0:
        group_len = group_len - 1

    def collect_group(block_slab, starting_block):
        blocks = []
        for inner in range(group_len):
            if not (starting_block and inner == 0):
                block_slab = shifted(block_slab, "ex", 1)
            blocks.append(block_slab)
        return (block_slab, blocks)

    def group_scoring(table, blocks, initial_round):
        tile = tile_scoring(jnp.concatenate(blocks, axis=0), training_gradient_rows)
        for inner in range(group_len):
            source = (position - initial_round - inner) % cycle_size
            piece = tile[inner * block_rows : (inner + 1) * block_rows]
            table = place_tile(table, piece, source * block_rows)
        return table

    block_slab, blocks = collect_group(precond, True)
    table = group_scoring(empty, blocks, 0)

    def advance(group, carry):
        block_slab, table = carry
        block_slab, blocks = collect_group(block_slab, False)
        return (block_slab, group_scoring(table, blocks, group * group_len))

    block_slab, table = lax.fori_loop(1, cycle_size // group_len, advance, (block_slab, table))
    return lax.psum_scatter(
        table.astype(jnp.bfloat16), "lay", scatter_dimension=0, tiled=True
    ).astype(jnp.float32)


def solution(mesh):
    return jax.shard_map(
        body,
        mesh=mesh,
        in_specs=(
            P("ex", "lay", None),
            P("ex", "lay", None),
            P("lay", None, None),
            P("lay", None, None),
        ),
        out_specs=P("lay", "ex"),
        check_vma=False,
    )
```

profile of v0, /device:TPU:1, one launch (start us, length us, event | category | flops | bytes accessed | tf_op | source)
XLA Modules:
  0.0 572.2 jit_solution(17873026514850246793)
XLA Ops:
  6.5 0.0 copy-start
  6.5 0.0 reduce-scatter.2.cloned.1.call-start
  6.5 4.9 copy.10
  11.5 0.0 copy-done
  11.5 0.0 copy-start.3
  11.5 2.6 fusion.23
  14.1 0.0 copy-done.3
  14.1 5.9 %fusion.25 = bf16[2,128,64,64]{1,3,2,0:T(8,128)(2,1)S(1)} fusion(f32[2,128,64,64]{1,3,2,0:T(8,128)S(1)} %fusion.23, f32[2,64,64]{2,1,0:T(8,128)S(1)} %copy-done.3), kind=kOutput, calls=%fused_computation.29 | convolution fusion | flops 806354944 | bytes 6324224 | tf_op jit(solution)/shard_map/tlac,lcd->tlad/dot_general | solution.py:32
  20.0 2.8 copy.12
  22.8 3.0 collective-permute-start.4
  25.8 23.3 %collective-permute-done.4 = bf16[128,2,4096]{2,0,1:T(8,128)(2,1)S(1)} collective-permute-done((bf16[128,2,4096]{2,0,1:T(8,128)(2,1)}, bf16[128,2,4096]{2,0,1:T(8,128)(2,1)S(1)}, u32[]{:S(2)}, u32[]{:S(2)}) %collective-permute-start.4) | collective-permute-done | bytes 2097184 | tf_op jit(solution)/shard_map/ppermute | solution.py:10
  49.1 0.0 copy-start.6
  49.1 1.3 copy-done.6
  50.4 2.4 collective-permute-start.5
  52.8 23.0 %collective-permute-done.5 = bf16[128,2,4096]{2,0,1:T(8,128)(2,1)} collective-permute-done((bf16[128,2,4096]{2,0,1:T(8,128)(2,1)S(1)}, bf16[128,2,4096]{2,0,1:T(8,128)(2,1)}, u32[]{:S(2)}, u32[]{:S(2)}) %collective-permute-start.5) | collective-permute-done | bytes 2097184 | tf_op jit(solution)/shard_map/ppermute | solution.py:10
  75.8 2.6 collective-permute-start.6
  78.4 12.8 %copy.14 = bf16[512,2,4096]{2,0,1:T(8,128)(2,1)} copy(bf16[512,2,4096]{2,1,0:T(2,128)(2,1)} %param.6) | data formatting | bytes 16777216 | tf_op args[0]
  91.2 10.5 %collective-permute-done.6 = bf16[128,2,4096]{2,0,1:T(8,128)(2,1)} collective-permute-done((bf16[128,2,4096]{2,0,1:T(8,128)(2,1)}, bf16[128,2,4096]{2,0,1:T(8,128)(2,1)}, u32[]{:S(2)}, u32[]{:S(2)}) %collective-permute-start.6) | collective-permute-done | bytes 2097184 | tf_op jit(solution)/shard_map/ppermute | solution.py:10
  101.6 0.0 copy-done.2
  101.7 13.1 %fusion.28 = bf16[2,512,512]{2,1,0:T(8,128)(2,1)S(1)} fusion(bf16[128,2,4096]{2,0,1:T(8,128)(2,1)} %collective-permute-done.6, bf16[128,2,4096]{2,0,1:T(8,128)(2,1)} %collective-permute-done.5, bf16[128,2,4096]{2,0,1:T(8,128)(2,1)} %copy-done.6, bf16[128,2,4096]{2,0,1:T(8,128)(2,1)S(1)} %copy-done.2, bf16[512,2,4096]{2,1,0:T(2,128)(2,1)} %param.6), kind=kOutput, calls=%fused_computation.30 | convolution fusion | flops 4329046016 | bytes 17825792 | tf_op jit(solution)/shard_map/aec,jec->eaj/dot_general | solution.py:14
  114.8 0.2 convert_reduce_fusion.1
  115.0 0.1 broadcast_in_dim.3
  115.2 371.5 %while.17 = (s32[]{:T(128)}, bf16[128,2,4096]{2,0,1:T(8,128)(2,1)}, bf16[2048,512]{1,0:T(8,128)(2,1)S(1)}, bf16[512,2,4096]{2,0,1:T(8,128)(2,1)}, s32[]{:T(128)}...) while((s32[]{:T(128)}, bf16[128,2,4096]{2,0,1:T(8,128)(2,1)}, ...), condition=%wide.region_3.4_spmd, body=%wide.region_1.3_spmd.sunk | while | flops 4329832448 | bytes 70779936 | solution.py:65
  115.2 2.6 collective-permute-start
  117.8 23.3 %collective-permute-done = bf16[128,2,4096]{2,0,1:T(8,128)(2,1)S(1)} collective-permute-done((bf16[128,2,4096]{2,0,1:T(8,128)(2,1)}, bf16[128,2,4096]{2,0,1:T(8,128)(2,1)S(1)}, u32[]{:S(2)}, u32[]{:S(2)}) %collective-permute-start) | collective-permute-done | bytes 2097184 | tf_op jit(solution)/shard_map/while/body/eval_jaxpr/ppermute | solution.py:10
  141.1 1.3 copy-done.4
  142.4 2.4 collective-permute-start.1
  144.8 23.0 %collective-permute-done.1 = bf16[128,2,4096]{2,0,1:T(8,128)(2,1)S(1)} collective-permute-done((bf16[128,2,4096]{2,0,1:T(8,128)(2,1)S(1)}, bf16[128,2,4096]{2,0,1:T(8,128)(2,1)S(1)}, u32[]{:S(2)}, u32[]{:S(2)}) %collective-permute-start.1) | collective-permute-done | bytes 2097184 | tf_op jit(solution)/shard_map/while/body/eval_jaxpr/ppermute | solution.py:10
  167.7 1.3 copy-done.5
  169.1 2.5 collective-permute-start.2
  171.5 23.0 %collective-permute-done.2 = bf16[128,2,4096]{2,0,1:T(8,128)(2,1)} collective-permute-done((bf16[128,2,4096]{2,0,1:T(8,128)(2,1)S(1)}, bf16[128,2,4096]{2,0,1:T(8,128)(2,1)}, u32[]{:S(2)}, u32[]{:S(2)}) %collective-permute-start.2) | collective-permute-done | bytes 2097184 | tf_op jit(solution)/shard_map/while/body/eval_jaxpr/ppermute | solution.py:10
  194.5 2.6 collective-permute-start.3
  197.1 24.7 %collective-permute-done.3 = bf16[128,2,4096]{2,0,1:T(8,128)(2,1)} collective-permute-done((bf16[128,2,4096]{2,0,1:T(8,128)(2,1)}, bf16[128,2,4096]{2,0,1:T(8,128)(2,1)}, u32[]{:S(2)}, u32[]{:S(2)}) %collective-permute-start.3) | collective-permute-done | bytes 2097184 | tf_op jit(solution)/shard_map/while/body/eval_jaxpr/ppermute | solution.py:10
  221.8 8.2 %fusion.41 = bf16[2,512,512]{2,1,0:T(8,128)(2,1)S(1)} fusion(bf16[512,2,4096]{2,0,1:T(8,128)(2,1)} %get-tuple-element.226, bf16[128,2,4096]{2,0,1:T(8,128)(2,1)} %collective-permute-done.3, bf16[128,2,4096]{2,0,1:T(8,128)(2,1)} %collective-permute-done.2, bf16[128,2,4096]{2,0,1:T(8,128)(2,1)} %copy-done.5, bf16[128,2,4096]{2,0,1:T(8,128)(2,1)} %copy-done.4), kind=kOutput, calls=%fused_computation.9.clone.1 | convolution fusion | flops 4329046016 | bytes 17825792 | tf_op jit(solution)/shard_map/while/body/eval_jaxpr/aec,jec->eaj/dot_general | solution.py:14
  230.1 0.2 convert_reduce_fusion.3
  230.4 1.1 collective-permute-start
  231.5 28.2 %collective-permute-done = bf16[128,2,4096]{2,0,1:T(8,128)(2,1)S(1)} collective-permute-done((bf16[128,2,4096]{2,0,1:T(8,128)(2,1)}, bf16[128,2,4096]{2,0,1:T(8,128)(2,1)S(1)}, u32[]{:S(2)}, u32[]{:S(2)}) %collective-permute-start) | collective-permute-done | bytes 2097184 | tf_op jit(solution)/shard_map/while/body/eval_jaxpr/ppermute | solution.py:10
  259.7 1.3 copy-done.4
  261.0 0.0 collective-permute-start.1
  261.0 29.1 %collective-permute-done.1 = bf16[128,2,4096]{2,0,1:T(8,128)(2,1)S(1)} collective-permute-done((bf16[128,2,4096]{2,0,1:T(8,128)(2,1)S(1)}, bf16[128,2,4096]{2,0,1:T(8,128)(2,1)S(1)}, u32[]{:S(2)}, u32[]{:S(2)}) %collective-permute-start.1) | collective-permute-done | bytes 2097184 | tf_op jit(solution)/shard_map/while/body/eval_jaxpr/ppermute | solution.py:10
  290.1 1.3 copy-done.5
  291.4 0.0 collective-permute-start.2
  291.4 29.2 %collective-permute-done.2 = bf16[128,2,4096]{2,0,1:T(8,128)(2,1)} collective-permute-done((bf16[128,2,4096]{2,0,1:T(8,128)(2,1)S(1)}, bf16[128,2,4096]{2,0,1:T(8,128)(2,1)}, u32[]{:S(2)}, u32[]{:S(2)}) %collective-permute-start.2) | collective-permute-done | bytes 2097184 | tf_op jit(solution)/shard_map/while/body/eval_jaxpr/ppermute | solution.py:10
  320.6 0.0 collective-permute-start.3
  320.6 29.4 %collective-permute-done.3 = bf16[128,2,4096]{2,0,1:T(8,128)(2,1)} collective-permute-done((bf16[128,2,4096]{2,0,1:T(8,128)(2,1)}, bf16[128,2,4096]{2,0,1:T(8,128)(2,1)}, u32[]{:S(2)}, u32[]{:S(2)}) %collective-permute-start.3) | collective-permute-done | bytes 2097184 | tf_op jit(solution)/shard_map/while/body/eval_jaxpr/ppermute | solution.py:10
  350.0 8.2 %fusion.41 = bf16[2,512,512]{2,1,0:T(8,128)(2,1)S(1)} fusion(bf16[512,2,4096]{2,0,1:T(8,128)(2,1)} %get-tuple-element.226, bf16[128,2,4096]{2,0,1:T(8,128)(2,1)} %collective-permute-done.3, bf16[128,2,4096]{2,0,1:T(8,128)(2,1)} %collective-permute-done.2, bf16[128,2,4096]{2,0,1:T(8,128)(2,1)} %copy-done.5, bf16[128,2,4096]{2,0,1:T(8,128)(2,1)} %copy-done.4), kind=kOutput, calls=%fused_computation.9.clone.1 | convolution fusion | flops 4329046016 | bytes 17825792 | tf_op jit(solution)/shard_map/while/body/eval_jaxpr/aec,jec->eaj/dot_general | solution.py:14
  358.2 0.2 convert_reduce_fusion.3
  358.5 0.1 collective-permute-start
  358.6 29.2 %collective-permute-done = bf16[128,2,4096]{2,0,1:T(8,128)(2,1)S(1)} collective-permute-done((bf16[128,2,4096]{2,0,1:T(8,128)(2,1)}, bf16[128,2,4096]{2,0,1:T(8,128)(2,1)S(1)}, u32[]{:S(2)}, u32[]{:S(2)}) %collective-permute-start) | collective-permute-done | bytes 2097184 | tf_op jit(solution)/shard_map/while/body/eval_jaxpr/ppermute | solution.py:10
  387.9 1.3 copy-done.4
  389.2 0.0 collective-permute-start.1
  389.2 29.1 %collective-permute-done.1 = bf16[128,2,4096]{2,0,1:T(8,128)(2,1)S(1)} collective-permute-done((bf16[128,2,4096]{2,0,1:T(8,128)(2,1)S(1)}, bf16[128,2,4096]{2,0,1:T(8,128)(2,1)S(1)}, u32[]{:S(2)}, u32[]{:S(2)}) %collective-permute-start.1) | collective-permute-done | bytes 2097184 | tf_op jit(solution)/shard_map/while/body/eval_jaxpr/ppermute | solution.py:10
  418.2 1.3 copy-done.5
  419.6 0.0 collective-permute-start.2
  419.6 29.2 %collective-permute-done.2 = bf16[128,2,4096]{2,0,1:T(8,128)(2,1)} collective-permute-done((bf16[128,2,4096]{2,0,1:T(8,128)(2,1)S(1)}, bf16[128,2,4096]{2,0,1:T(8,128)(2,1)}, u32[]{:S(2)}, u32[]{:S(2)}) %collective-permute-start.2) | collective-permute-done | bytes 2097184 | tf_op jit(solution)/shard_map/while/body/eval_jaxpr/ppermute | solution.py:10
  448.8 0.0 collective-permute-start.3
  448.8 29.4 %collective-permute-done.3 = bf16[128,2,4096]{2,0,1:T(8,128)(2,1)} collective-permute-done((bf16[128,2,4096]{2,0,1:T(8,128)(2,1)}, bf16[128,2,4096]{2,0,1:T(8,128)(2,1)}, u32[]{:S(2)}, u32[]{:S(2)}) %collective-permute-start.3) | collective-permute-done | bytes 2097184 | tf_op jit(solution)/shard_map/while/body/eval_jaxpr/ppermute | solution.py:10
  478.2 8.2 %fusion.41 = bf16[2,512,512]{2,1,0:T(8,128)(2,1)S(1)} fusion(bf16[512,2,4096]{2,0,1:T(8,128)(2,1)} %get-tuple-element.226, bf16[128,2,4096]{2,0,1:T(8,128)(2,1)} %collective-permute-done.3, bf16[128,2,4096]{2,0,1:T(8,128)(2,1)} %collective-permute-done.2, bf16[128,2,4096]{2,0,1:T(8,128)(2,1)} %copy-done.5, bf16[128,2,4096]{2,0,1:T(8,128)(2,1)} %copy-done.4), kind=kOutput, calls=%fused_computation.9.clone.1 | convolution fusion | flops 4329046016 | bytes 17825792 | tf_op jit(solution)/shard_map/while/body/eval_jaxpr/aec,jec->eaj/dot_general | solution.py:14
  486.4 0.2 convert_reduce_fusion.3
  486.7 0.0 copy-start.1
  486.7 1.3 copy-done.1
  488.0 0.0 reduce-scatter.2.cloned.1.call-update
  488.1 75.5 %reduce-scatter.2.cloned.1.call-done = bf16[256,512]{1,0:T(8,128)(2,1)} async-done(((bf16[2048,512]{1,0:T(8,128)(2,1)}), bf16[256,512]{1,0:T(8,128)(2,1)}) %reduce-scatter.2.cloned.1.call-update) | async-done | bytes 262160 | tf_op jit(solution)/shard_map/reduce_scatter | solution.py:66
  563.5 1.8 convert_element_type.48
  (23 shorter events, 0.3 us)
Async XLA Ops:
  6.5 4.9 copy-start
  6.5 557.0 %reduce-scatter.2.cloned.1.call-start = ((), (), s32[]{:S(2)}) async-start(), calls=%async_computation.1 | async-start | bytes 2359296 | tf_op jit(solution)/shard_map/reduce_scatter | solution.py:66
  11.5 2.7 copy-start.3
  22.8 26.3 %collective-permute-start.4 = (bf16[128,2,4096]{2,0,1:T(8,128)(2,1)}, bf16[128,2,4096]{2,0,1:T(8,128)(2,1)S(1)}, u32[]{:S(2)}, u32[]{:S(2)}) collective-permute-start(bf16[128,2,4096]{2,0,1:T(8,128)(2,1)} %copy.12), channel_id=1, source_target_pairs={{0,8},{8,16},{16,24},{24,32},{32,40},{40,48},{48,56},{56,64},{64,7... | collective-permute-start | bytes 6291464 | tf_op jit(solution)/shard_map/ppermute | solution.py:10
  49.1 1.3 copy-start.6
  50.4 25.4 %collective-permute-start.5 = (bf16[128,2,4096]{2,0,1:T(8,128)(2,1)S(1)}, bf16[128,2,4096]{2,0,1:T(8,128)(2,1)}, u32[]{:S(2)}, u32[]{:S(2)}) collective-permute-start(bf16[128,2,4096]{2,0,1:T(8,128)(2,1)S(1)} %collective-permute-done.4), channel_id=1, source_target_pairs={{0,8},{8,16},{16,24},{24,32},{32,40},{40,48},{48,56},{56,64},{64,7... | collective-permute-start | bytes 6291464 | tf_op jit(solution)/shard_map/ppermute | solution.py:10
  75.8 25.9 %collective-permute-start.6 = (bf16[128,2,4096]{2,0,1:T(8,128)(2,1)}, bf16[128,2,4096]{2,0,1:T(8,128)(2,1)}, u32[]{:S(2)}, u32[]{:S(2)}) collective-permute-start(bf16[128,2,4096]{2,0,1:T(8,128)(2,1)} %collective-permute-done.5), channel_id=1, source_target_pairs={{0,8},{8,16},{16,24},{24,32},{32,40},{40,48},{48,56},{56,64},{64,7... | collective-permute-start | bytes 6291464 | tf_op jit(solution)/shard_map/ppermute | solution.py:10
  78.4 23.3 %copy-start.2 = (bf16[128,2,4096]{2,0,1:T(8,128)(2,1)S(1)}, bf16[128,2,4096]{2,0,1:T(8,128)(2,1)}, u32[]{:S(2)}) copy-start(bf16[128,2,4096]{2,0,1:T(8,128)(2,1)} %copy.12) | copy-start | bytes 6291460
  115.2 25.9 %collective-permute-start = (bf16[128,2,4096]{2,0,1:T(8,128)(2,1)}, bf16[128,2,4096]{2,0,1:T(8,128)(2,1)S(1)}, u32[]{:S(2)}, u32[]{:S(2)}) collective-permute-start(bf16[128,2,4096]{2,0,1:T(8,128)(2,1)} %get-tuple-element.209), channel_id=1, source_target_pairs={{0,8},{8,16},{16,24},{24,32},{32,40},{40,48},{48,56},{56,64},{64,7... | collective-permute-start | bytes 6291464 | tf_op jit(solution)/shard_map/while/body/eval_jaxpr/ppermute | solution.py:10
  141.1 1.3 copy-start.4
  142.4 25.4 %collective-permute-start.1 = (bf16[128,2,4096]{2,0,1:T(8,128)(2,1)S(1)}, bf16[128,2,4096]{2,0,1:T(8,128)(2,1)S(1)}, u32[]{:S(2)}, u32[]{:S(2)}) collective-permute-start(bf16[128,2,4096]{2,0,1:T(8,128)(2,1)S(1)} %collective-permute-done), channel_id=1, source_target_pairs={{0,8},{8,16},{16,24},{24,32},{32,40},{40,48},{48,56},{56,64},{64,7... | collective-permute-start | bytes 6291464 | tf_op jit(solution)/shard_map/while/body/eval_jaxpr/ppermute | solution.py:10
  167.7 1.3 copy-start.5
  169.1 25.5 %collective-permute-start.2 = (bf16[128,2,4096]{2,0,1:T(8,128)(2,1)S(1)}, bf16[128,2,4096]{2,0,1:T(8,128)(2,1)}, u32[]{:S(2)}, u32[]{:S(2)}) collective-permute-start(bf16[128,2,4096]{2,0,1:T(8,128)(2,1)S(1)} %collective-permute-done.1), channel_id=1, source_target_pairs={{0,8},{8,16},{16,24},{24,32},{32,40},{40,48},{48,56},{56,64},{64,7... | collective-permute-start | bytes 6291464 | tf_op jit(solution)/shard_map/while/body/eval_jaxpr/ppermute | solution.py:10
  194.5 27.3 %collective-permute-start.3 = (bf16[128,2,4096]{2,0,1:T(8,128)(2,1)}, bf16[128,2,4096]{2,0,1:T(8,128)(2,1)}, u32[]{:S(2)}, u32[]{:S(2)}) collective-permute-start(bf16[128,2,4096]{2,0,1:T(8,128)(2,1)} %collective-permute-done.2), channel_id=1, source_target_pairs={{0,8},{8,16},{16,24},{24,32},{32,40},{40,48},{48,56},{56,64},{64,7... | collective-permute-start | bytes 6291464 | tf_op jit(solution)/shard_map/while/body/eval_jaxpr/ppermute | solution.py:10
  230.4 29.3 %collective-permute-start = (bf16[128,2,4096]{2,0,1:T(8,128)(2,1)}, bf16[128,2,4096]{2,0,1:T(8,128)(2,1)S(1)}, u32[]{:S(2)}, u32[]{:S(2)}) collective-permute-start(bf16[128,2,4096]{2,0,1:T(8,128)(2,1)} %get-tuple-element.209), channel_id=1, source_target_pairs={{0,8},{8,16},{16,24},{24,32},{32,40},{40,48},{48,56},{56,64},{64,7... | collective-permute-start | bytes 6291464 | tf_op jit(solution)/shard_map/while/body/eval_jaxpr/ppermute | solution.py:10
  259.7 1.3 copy-start.4
  261.0 29.1 %collective-permute-start.1 = (bf16[128,2,4096]{2,0,1:T(8,128)(2,1)S(1)}, bf16[128,2,4096]{2,0,1:T(8,128)(2,1)S(1)}, u32[]{:S(2)}, u32[]{:S(2)}) collective-permute-start(bf16[128,2,4096]{2,0,1:T(8,128)(2,1)S(1)} %collective-permute-done), channel_id=1, source_target_pairs={{0,8},{8,16},{16,24},{24,32},{32,40},{40,48},{48,56},{56,64},{64,7... | collective-permute-start | bytes 6291464 | tf_op jit(solution)/shard_map/while/body/eval_jaxpr/ppermute | solution.py:10
  290.1 1.3 copy-start.5
  291.4 29.2 %collective-permute-start.2 = (bf16[128,2,4096]{2,0,1:T(8,128)(2,1)S(1)}, bf16[128,2,4096]{2,0,1:T(8,128)(2,1)}, u32[]{:S(2)}, u32[]{:S(2)}) collective-permute-start(bf16[128,2,4096]{2,0,1:T(8,128)(2,1)S(1)} %collective-permute-done.1), channel_id=1, source_target_pairs={{0,8},{8,16},{16,24},{24,32},{32,40},{40,48},{48,56},{56,64},{64,7... | collective-permute-start | bytes 6291464 | tf_op jit(solution)/shard_map/while/body/eval_jaxpr/ppermute | solution.py:10
  320.6 29.4 %collective-permute-start.3 = (bf16[128,2,4096]{2,0,1:T(8,128)(2,1)}, bf16[128,2,4096]{2,0,1:T(8,128)(2,1)}, u32[]{:S(2)}, u32[]{:S(2)}) collective-permute-start(bf16[128,2,4096]{2,0,1:T(8,128)(2,1)} %collective-permute-done.2), channel_id=1, source_target_pairs={{0,8},{8,16},{16,24},{24,32},{32,40},{40,48},{48,56},{56,64},{64,7... | collective-permute-start | bytes 6291464 | tf_op jit(solution)/shard_map/while/body/eval_jaxpr/ppermute | solution.py:10
  358.5 29.3 %collective-permute-start = (bf16[128,2,4096]{2,0,1:T(8,128)(2,1)}, bf16[128,2,4096]{2,0,1:T(8,128)(2,1)S(1)}, u32[]{:S(2)}, u32[]{:S(2)}) collective-permute-start(bf16[128,2,4096]{2,0,1:T(8,128)(2,1)} %get-tuple-element.209), channel_id=1, source_target_pairs={{0,8},{8,16},{16,24},{24,32},{32,40},{40,48},{48,56},{56,64},{64,7... | collective-permute-start | bytes 6291464 | tf_op jit(solution)/shard_map/while/body/eval_jaxpr/ppermute | solution.py:10
  387.9 1.3 copy-start.4
  389.2 29.1 %collective-permute-start.1 = (bf16[128,2,4096]{2,0,1:T(8,128)(2,1)S(1)}, bf16[128,2,4096]{2,0,1:T(8,128)(2,1)S(1)}, u32[]{:S(2)}, u32[]{:S(2)}) collective-permute-start(bf16[128,2,4096]{2,0,1:T(8,128)(2,1)S(1)} %collective-permute-done), channel_id=1, source_target_pairs={{0,8},{8,16},{16,24},{24,32},{32,40},{40,48},{48,56},{56,64},{64,7... | collective-permute-start | bytes 6291464 | tf_op jit(solution)/shard_map/while/body/eval_jaxpr/ppermute | solution.py:10
  418.2 1.3 copy-start.5
  419.6 29.2 %collective-permute-start.2 = (bf16[128,2,4096]{2,0,1:T(8,128)(2,1)S(1)}, bf16[128,2,4096]{2,0,1:T(8,128)(2,1)}, u32[]{:S(2)}, u32[]{:S(2)}) collective-permute-start(bf16[128,2,4096]{2,0,1:T(8,128)(2,1)S(1)} %collective-permute-done.1), channel_id=1, source_target_pairs={{0,8},{8,16},{16,24},{24,32},{32,40},{40,48},{48,56},{56,64},{64,7... | collective-permute-start | bytes 6291464 | tf_op jit(solution)/shard_map/while/body/eval_jaxpr/ppermute | solution.py:10
  448.8 29.4 %collective-permute-start.3 = (bf16[128,2,4096]{2,0,1:T(8,128)(2,1)}, bf16[128,2,4096]{2,0,1:T(8,128)(2,1)}, u32[]{:S(2)}, u32[]{:S(2)}) collective-permute-start(bf16[128,2,4096]{2,0,1:T(8,128)(2,1)} %collective-permute-done.2), channel_id=1, source_target_pairs={{0,8},{8,16},{16,24},{24,32},{32,40},{40,48},{48,56},{56,64},{64,7... | collective-permute-start | bytes 6291464 | tf_op jit(solution)/shard_map/while/body/eval_jaxpr/ppermute | solution.py:10
  486.7 1.3 copy-start.1
Sparse Core Ops, SparseCore 0:
  488.2 75.3 reduce-scatter.1
where the time goes:
time: 572 us
  waiting for transfers between devices  459 us (80%)
  matrix products  46.3 us (8%)
  local copies, waits for them, and re-layouts  31.4 us (5%)
  starting transfers between devices  19.2 us (3%)
  between operations  13.5 us (2%)
    ppermute x15, waiting for transfers between devices, shifted(): return lax.ppermute(value, axis, pairs)  383 us
    reduce_scatter x1, waiting for transfers between devices, body(): lax.psum_scatter(table.astype(jnp.bfloat16), 'lay', scatter_dimension=0,...  75.5 us
    dot_general x4, matrix products, tile_scoring(): jnp.einsum('aec,jec->eaj', block_slab, training_gradient_rows, preferred_...  37.9 us
    unnamed x12, local copies, waits for them, and re-layouts  20.4 us
    ppermute x15, starting transfers between devices, shifted(): return lax.ppermute(value, axis, pairs)  19.2 us
  transfers between devices with their start and end apart: 16, of which 16 were waited for; matrix products, arithmetic and copies ran while one was open for 2% of the time, Pallas kernels for 0%

commit v1 on v0

v1 whole, which is shorter than its diff:
```python
import functools

import jax
import jax.numpy as jnp
from jax import lax
from jax.experimental import pallas as pl
from jax.experimental.pallas import tpu as pltpu
from jax.sharding import PartitionSpec as P

BF, F32 = jnp.bfloat16, jnp.float32
NT = (((1,), (1,)), ((), ()))
TN = (((0,), (0,)), ((), ()))
HIGHEST = lax.Precision.HIGHEST

SLOTS = ((0, 0), (1, 0), (0, 3), (0, 1), (1, 3), (1, 1), (0, 2), (1, 2))
PIECES = 8
HEAD = 32
ROWS = 16
STEPS = 6
TREE_STEP = 2
PART = 512


def iota(shape, dim):
    return lax.broadcasted_iota(jnp.int32, shape, dim)


def kernel(train, test, inv_out, inv_in, out, g1, g2, bmat, stage, amat, weight, cs, yr, xs, xr, ysum,
           r1, r1s, s1, r2, r2h, r2s, s2, ysem, ysend, xsem, xsend, local):
    ex, lay = lax.axis_index("ex"), lax.axis_index("lay")
    xh, z, c = ex // 8, (ex // 2) % 4, ex % 2
    y, xl = lay // 2, lay % 2

    def at(xh_, z_, c_):
        return (xh_ * 8 + z_ * 2 + c_, lay)

    zup, zdown = lax.rem(z + 1, 4), lax.rem(z + 3, 4)
    to_x, to_up, to_down, to_s = at(1 - xh, z, c), at(xh, zup, c), at(xh, zdown, c), at(xh, z, 1 - c)
    to_y = [(ex, lax.rem(y + d, 4) * 2 + xl) for d in (1, 2, 3)]
    to_xl = (ex, y * 2 + 1 - xl)

    def remote(src, dst, send, recv, device):
        return pltpu.make_async_remote_copy(src_ref=src, dst_ref=dst, send_sem=send, recv_sem=recv,
                                            device_id=device, device_id_type=pl.DeviceIdType.MESH)

    def arrived(ref, recv):
        remote(ref, ref, s1.at[0, 0], recv, to_x).wait_recv()

    def left(ref, send):
        remote(ref, ref, send, r1.at[0, 0], to_x).wait_send()

    def fetch(i):
        if i < 0:
            src = test.reshape(256, 4096)
        else:
            src = train.reshape(1024, 4096).at[pl.ds(i * 256, 256)]
        return pltpu.make_async_copy(src, stage.at[(i + 1) % 2], local.at[(i + 1) % 2])

    fetch(-1).start()
    fetch(0).start()
    barrier = pltpu.get_barrier_semaphore()
    for device in [to_x, to_up, to_down, to_s, to_xl] + to_y:
        pl.semaphore_signal(barrier, inc=1, device_id=device, device_id_type=pl.DeviceIdType.MESH)

    def split_layers(slot, write):
        ri, ci = iota((256, 256), 0), iota((256, 256), 1)
        order = (ci == 2 * (ri % 128) + ri // 128).astype(BF)

        @pl.loop(0, 8)
        def _(i):
            cols = pl.ds(pl.multiple_of(i * 512, 512), 512)
            write(cols, jnp.dot(order, stage[slot, :, cols], preferred_element_type=F32).astype(BF))

    def write_a(cols, value):
        amat[0, :, cols] = value[:128]
        amat[1, :, cols] = value[128:]

    fetch(-1).wait()
    split_layers(0, write_a)
    fetch(1).start()
    pl.semaphore_wait(barrier, 8)

    def precondition(l, j):
        r, col = iota((64, PART), 0), iota((64, PART), 1)
        e = lax.dot_general(inv_out[l], (r == (PART // 64) * j + col // 64).astype(F32), TN,
                            precision=HIGHEST, preferred_element_type=F32)
        f = jnp.dot(inv_in[l], (r == col % 64).astype(F32), precision=HIGHEST, preferred_element_type=F32)
        weight[...] = (e[:, None, :] * f[None]).astype(BF).reshape(4096, PART)
        return jnp.dot(amat[l], weight[...], preferred_element_type=F32).astype(BF)

    def own1(p):
        ref = g1.at[p, 0]
        remote(ref, g1.at[p, 1], s1.at[p, 0], r1.at[p, 1], to_x).start()
        remote(ref, g1.at[p, 2], s1.at[p, 1], r1.at[p, 2], to_up).start()
        remote(ref, g1.at[p, 3], s1.at[p, 2], r1.at[p, 3], to_down).start()

    def first1(p):
        h = lax.rem(p, 2)
        arrived(g1.at[p, 1], r1.at[p, 1])
        remote(g1.at[p, 1], g1.at[p, 4], s1.at[p, 3], r1.at[p, 4], to_up).start()
        remote(g1.at[p, 1], g1.at[p, 5], s1.at[p, 4], r1.at[p, 5], to_down).start()
        arrived(g1.at[p, 2], r1.at[p, 2])
        arrived(g1.at[p, 3], r1.at[p, 3])
        onward = (jnp.where(h == 0, to_up[0], to_down[0]), lay)
        remote(g1.at[p, 2 + h], g1.at[p, 6], s1.at[p, 5], r1.at[p, 6], onward).start()
        remote(g1.at[p, pl.ds(0, 4)], g1.at[p, pl.ds(8, 4)], s1.at[p, 6], r1s.at[p, 0], to_s).start()

    def second1(p):
        arrived(g1.at[p, 6], r1.at[p, 6])
        remote(g1.at[p, 6], g1.at[p, 7], s1.at[p, 7], r1.at[p, 7], to_x).start()
        arrived(g1.at[p, 4], r1.at[p, 4])
        arrived(g1.at[p, 5], r1.at[p, 5])

    def third1(p):
        arrived(g1.at[p, 7], r1.at[p, 7])
        remote(g1.at[p, pl.ds(4, 4)], g1.at[p, pl.ds(12, 4)], s1.at[p, 8], r1s.at[p, 1], to_s).start()

    def drain1(p):
        for k in (0, 1, 2, 3, 4, 5, 7):
            left(g1.at[p, 0], s1.at[p, k])
        for k, group in ((6, 0), (8, 1)):
            left(g1.at[p, pl.ds(0, 4)], s1.at[p, k])
            arrived(g1.at[p, pl.ds(8 + 4 * group, 4)], r1s.at[p, group])

    def own2(i):
        ref = g2.at[i, 0]
        remote(ref, g2.at[i, 1], s2.at[i, 0], r2.at[i, 1], to_x).start()
        remote(ref, g2.at[i, 2], s2.at[i, 1], r2.at[i, 2], to_up).start()
        remote(ref, g2.at[i, 3], s2.at[i, 2], r2.at[i, 3], to_down).start()

    def first2(i):
        tree = i == TREE_STEP
        arrived(g2.at[i, 1], r2.at[i, 1])

        @pl.when(jnp.logical_not(tree))
        def _():
            remote(g2.at[i, 1], g2.at[i, 4], s2.at[i, 3], r2.at[i, 4], to_up).start()
            remote(g2.at[i, 1], g2.at[i, 5], s2.at[i, 4], r2.at[i, 5], to_down).start()

        arrived(g2.at[i, 2], r2.at[i, 2])
        remote(g2.at[i, 2, 0], g2.at[i, 6, 0], s2.at[i, 5], r2h.at[i, 0, 0], to_up).start()
        arrived(g2.at[i, 3], r2.at[i, 3])
        remote(g2.at[i, 3, 1], g2.at[i, 6, 1], s2.at[i, 6], r2h.at[i, 0, 1], to_down).start()

        @pl.when(tree)
        def _():
            remote(g2.at[i, 2], g2.at[i, 4], s2.at[i, 3], r2.at[i, 4], to_x).start()
            remote(g2.at[i, 3], g2.at[i, 5], s2.at[i, 4], r2.at[i, 5], to_x).start()

        remote(g2.at[i, pl.ds(0, 4)], g2.at[i, pl.ds(8, 4)], s2.at[i, 7], r2s.at[i, 0], to_s).start()

    def second2(i):
        for h in (0, 1):
            arrived(g2.at[i, 6, h], r2h.at[i, 0, h])
            remote(g2.at[i, 6, h], g2.at[i, 7, h], s2.at[i, 8 + h], r2h.at[i, 1, h], to_x).start()
        arrived(g2.at[i, 4], r2.at[i, 4])
        arrived(g2.at[i, 5], r2.at[i, 5])

    def third2(i):
        for h in (0, 1):
            arrived(g2.at[i, 7, h], r2h.at[i, 1, h])
        remote(g2.at[i, pl.ds(4, 4)], g2.at[i, pl.ds(12, 4)], s2.at[i, 10], r2s.at[i, 1], to_s).start()

    def fourth2(i):
        for group in (0, 1):
            arrived(g2.at[i, pl.ds(8 + 4 * group, 4)], r2s.at[i, group])

    def drain2(i):
        for k in (0, 1, 2, 3, 4):
            left(g2.at[i, 0], s2.at[i, k])
        for k in (5, 6, 8, 9):
            left(g2.at[i, 0, 0], s2.at[i, k])
        for k in (7, 10):
            left(g2.at[i, pl.ds(0, 4)], s2.at[i, k])

    def post(q, scores):
        for p in range(2):
            for k, (dx, dz) in enumerate(SLOTS):
                sx, sz = (1 - xh if dx else xh), lax.rem(z + dz, 4)
                row = pl.multiple_of(lax.rem(sz, 2) * 32 + (1 - c if p else c) * 16, 16)
                n = p * 8 + k
                cs[q, sx * 2 + sz // 2, pl.ds(row, 16), :] = scores[n * 16 : n * 16 + 16].astype(BF)
        for d in (1, 2, 3):
            remote(cs.at[q, lax.rem(y + d, 4)], yr.at[q, d - 1], ysend.at[q, d - 1], ysem.at[q, d - 1],
                   to_y[d - 1]).start()

    def over_y(q):
        total = cs[q, y].astype(F32)
        for d in range(3):
            arrived(yr.at[q, d], ysem.at[q, d])
            total += yr[q, d].astype(F32)
        ysum[q] = total.reshape(2, 32, 512)
        xs[q] = ysum[q, 1 - xl].astype(BF)
        remote(xs.at[q], xr.at[q], xsend.at[q], xsem.at[q], to_xl).start()

    def over_x(q):
        arrived(xr.at[q], xsem.at[q])
        total = ysum[q, xl] + xr[q].astype(F32)
        for k in range(2):
            out[pl.ds(pl.multiple_of(k * 128 + q * 16, 16), 16), :] = total[k * 16 : k * 16 + 16]

    def main_head(q):
        rows = pl.ds(pl.multiple_of(q * 16, 16), 16)
        scores = None
        for p in range(PIECES):
            lhs = g1[p, :, rows, :].reshape(256, 1024)
            part = lax.dot_general(lhs, bmat[p % 2, :, (p // 2) * 1024 : (p // 2 + 1) * 1024], NT,
                                   preferred_element_type=F32)
            scores = part if scores is None else scores + part
        post(q, scores)

    def main_step(i):
        scores = lax.dot_general(g2[i, :, 0].reshape(256, 4096), bmat[0], NT, preferred_element_type=F32)
        scores += lax.dot_general(g2[i, :, 1].reshape(256, 4096), bmat[1], NT, preferred_element_type=F32)
        post(i + 2, scores)

    @pl.loop(0, PIECES)
    def _(p):
        l, quarter = lax.rem(p, 2), p // 2

        @pl.loop(0, 2)
        def _(part):
            j = quarter * 2 + part
            value = precondition(l, j)
            g1[p, 0, :, pl.ds(pl.multiple_of(part * PART, PART), PART)] = value[:HEAD]
            cols = pl.ds(pl.multiple_of(j * PART, PART), PART)
            for i in range(STEPS):
                g2[i, 0, l, :, cols] = value[HEAD + i * ROWS : HEAD + (i + 1) * ROWS]

        own1(p)

        @pl.when(p >= 1)
        def _():
            first1(p - 1)

        @pl.when(p >= 2)
        def _():
            second1(p - 2)

        @pl.when(p >= 3)
        def _():
            third1(p - 3)

    last = PIECES - 1
    own2(0)
    first1(last)
    second1(last - 1)
    third1(last - 2)
    own2(1)
    second1(last)
    third1(last - 1)
    third1(last)

    @pl.loop(0, STEPS + 6)
    def _(t):
        @pl.when((t >= 2) & (t < STEPS))
        def _():
            own2(t)

        @pl.when((t >= 1) & (t < STEPS + 1))
        def _():
            first2(t - 1)

        @pl.when(t < 4)
        def _():
            slot = lax.rem(t + 1, 2)

            def write_b(cols, value):
                rows = pl.ds(pl.multiple_of(t * 128, 128), 128)
                bmat[0, rows, cols] = value[:128]
                bmat[1, rows, cols] = value[128:]

            pltpu.make_async_copy(train.reshape(1024, 4096).at[pl.ds(0, 256)], stage.at[slot], local.at[slot]).wait()
            split_layers(slot, write_b)

            @pl.when(t < 2)
            def _():
                start = pl.multiple_of((t + 2) * 256, 256)
                pltpu.make_async_copy(train.reshape(1024, 4096).at[pl.ds(start, 256)], stage.at[slot],
                                      local.at[slot]).start()

        @pl.when((t >= 2) & (t < STEPS + 2))
        def _():
            second2(t - 2)

        @pl.when((t >= 3) & (t < STEPS + 3))
        def _():
            third2(t - 3)

        @pl.when(t == 2)
        def _():
            @pl.loop(0, PIECES)
            def _(p):
                drain1(p)

        @pl.when(t == 3)
        def _():
            main_head(0)
            main_head(1)

        @pl.when((t >= 4) & (t < STEPS + 4))
        def _():
            fourth2(t - 4)
            main_step(t - 4)

        @pl.when(t == 4)
        def _():
            over_y(0)
            over_y(1)

        @pl.when((t >= 5) & (t < STEPS + 5))
        def _():
            over_y(t - 3)

        @pl.when(t == 5)
        def _():
            over_x(0)
            over_x(1)

        @pl.when(t >= 6)
        def _():
            drain2(t - 6)
            over_x(t - 4)

    @pl.loop(0, 8)
    def _(q):
        for d in range(3):
            left(cs.at[q, d], ysend.at[q, d])
        left(xs.at[q], xsend.at[q])


def body(train, test, inv_out, inv_in):
    vmem, hbm = pl.BlockSpec(memory_space=pltpu.VMEM), pl.BlockSpec(memory_space=pl.ANY)
    dma = pltpu.SemaphoreType.DMA
    return pl.pallas_call(
        kernel,
        out_shape=jax.ShapeDtypeStruct((256, 512), F32),
        in_specs=[hbm, hbm, vmem, vmem],
        out_specs=vmem,
        scratch_shapes=[
            pltpu.VMEM((PIECES, 16, HEAD, 1024), BF),
            pltpu.VMEM((STEPS, 16, 2, ROWS, 4096), BF),
            pltpu.VMEM((2, 512, 4096), BF),
            pltpu.VMEM((2, 256, 4096), BF),
            pltpu.VMEM((2, 128, 4096), BF),
            pltpu.VMEM((4096, PART), BF),
            pltpu.VMEM((8, 4, 64, 512), BF),
            pltpu.VMEM((8, 3, 64, 512), BF),
            pltpu.VMEM((8, 32, 512), BF),
            pltpu.VMEM((8, 32, 512), BF),
            pltpu.VMEM((8, 2, 32, 512), F32),
            dma((PIECES, 8)),
            dma((PIECES, 2)),
            dma((PIECES, 9)),
            dma((STEPS, 8)),
            dma((STEPS, 2, 2)),
            dma((STEPS, 2)),
            dma((STEPS, 11)),
            dma((8, 3)),
            dma((8, 3)),
            dma((8,)),
            dma((8,)),
            dma((2,)),
        ],
        compiler_params=pltpu.CompilerParams(
            collective_id=0, has_side_effects=True, vmem_limit_bytes=62 * 2**20
        ),
        cost_estimate=pl.CostEstimate(flops=26 * 10**9, bytes_accessed=12 * 2**20, transcendentals=0),
    )(train, test, inv_out, inv_in)


def solution(mesh):
    return jax.shard_map(
        body,
        mesh=mesh,
        in_specs=(P("ex", "lay", None), P("ex", "lay", None), P("lay", None, None), P("lay", None, None)),
        out_specs=P("lay", "ex"),
        check_vma=False,
    )
```

time: 572 us -> 154 us (0.27)
  waiting for transfers between devices: 459 us -> 0 us
  Pallas kernels: 0 us -> 151 us
  matrix products: 46.3 us -> 0 us
  local copies, waits for them, and re-layouts: 31.4 us -> 1.87 us
  starting transfers between devices: 19.2 us -> 0 us
  between operations: 13.5 us -> 0.01 us
    ppermute x15 -> x0, waiting for transfers between devices: 383 us -> none  [shifted(): return lax.ppermute(value, axis, pairs)]
    pallas_call x0 -> x1, Pallas kernels: none -> 151 us  [body(): pl.pallas_call(kernel, out_shape=jax.ShapeDtypeStruct((256, 512), F32), i...]
    reduce_scatter x1 -> x0, waiting for transfers between devices: 75.5 us -> none  [body(): lax.psum_scatter(table.astype(jnp.bfloat16), 'lay', scatter_dimension=0,...]
    dot_general x6 -> x0, matrix products: 46.3 us -> none  [the longest x4 37.9 us: tile_scoring(): jnp.einsum('aec,jec->eaj', block_slab, training_gradient_rows, preferred_...]
    ppermute x15 -> x0, starting transfers between devices: 19.2 us -> none  [shifted(): return lax.ppermute(value, axis, pairs)]
    unnamed x12 -> x1, local copies, waits for them, and re-layouts: 20.4 us -> 1.87 us
    while x12 -> x0, local copies, waits for them, and re-layouts: 7.89 us -> none
  transfers between devices with their start and end apart: 16 -> 0, of which waited for: 16 -> 0; matrix products, arithmetic and copies ran while one was open for 2% -> 0% of each run, Pallas kernels for 0% -> 0%
where the time goes in v1:
time: 154 us; the launch traced here: 153 us
  Pallas kernels  151 us (98%)
  local copies, waits for them, and re-layouts  1.87 us (1%)
    pallas_call x1, Pallas kernels, body(): pl.pallas_call(kernel, out_shape=jax.ShapeDtypeStruct((256, 512), F32), i...  151 us

profile of v1, /device:TPU:1, one launch (start us, length us, event | category | flops | bytes accessed | tf_op | source)
XLA Modules:
  0.0 152.8 jit_solution(3533361235705983339)
XLA Ops:
  0.0 150.9 %shard_map.46 = f32[256,512]{1,0:T(8,128)} custom-call(bf16[512,2,4096]{2,1,0:T(2,128)(2,1)} %train.1, bf16[128,2,4096]{2,1,0:T(2,128)(2,1)} %test.1, f32[2,64,64]{2,1,0:T(8,128)} %inv_out.1, f32[2,64,64]{2,1,0:T(8,128)} %inv_in.1), custom_call_target="tpu_custom_call" | custom-call | flops 25999998976 | bytes 12582912 | tf_op jit(solution)/shard_map/pallas_call | solution.py:335
  150.9 1.9 %copy.6 = f32[256,512]{1,0:T(8,128)} copy(f32[256,512]{1,0:T(8,128)} %shard_map.46) | data formatting | bytes 1048576

commit v2 on v0

v2 whole, which is shorter than its diff:
```python
import jax
import jax.numpy as jnp
from jax import lax
from jax.experimental import pallas as pl
from jax.experimental.pallas import tpu as pltpu
from jax.sharding import PartitionSpec as P

BF, F32 = jnp.bfloat16, jnp.float32
NT = (((1,), (1,)), ((), ()))
TN = (((0,), (0,)), ((), ()))
HIGHEST = lax.Precision.HIGHEST

SLOTS = ((0, 0), (1, 0), (0, 3), (0, 1), (1, 3), (1, 1), (0, 2), (1, 2))
PIECES = 8
HEAD = 64
ROWS = 16
ITEMS = 8
QUEUE = 8
PART = 512
CUT1, CUT2 = 896, 3584
RING = 5


def iota(shape, dim):
    return lax.broadcasted_iota(jnp.int32, shape, dim)


def kernel(train, test, inv_out, inv_in, out, g1, g2, bmat, stage, amat, weight, cs, yr, xs, xr, ysum, zr, acc,
           r1, r1h, r1c, r1s, r2, r2h, r2c, r2s, s2, ysem, ysend, xsem, xsend, zsem, zsend, local):
    ex, lay = lax.axis_index("ex"), lax.axis_index("lay")
    xh, z, c = ex // 8, (ex // 2) % 4, ex % 2
    y, xl = lay // 2, lay % 2

    def at(xh_, z_, c_):
        return (xh_ * 8 + z_ * 2 + c_, lay)

    to_x, to_s = at(1 - xh, z, c), at(xh, z, 1 - c)
    to_up, to_down = at(xh, lax.rem(z + 1, 4), c), at(xh, lax.rem(z + 3, 4), c)
    others = [(d, f) for f in (0, 1) for d in range(4) if d or f]
    to_lay = {(d, f): (ex, lax.rem(y + d, 4) * 2 + (1 - xl if f else xl)) for d, f in others}

    def remote(src, dst, send, recv, device):
        return pltpu.make_async_remote_copy(src_ref=src, dst_ref=dst, send_sem=send, recv_sem=recv,
                                            device_id=device, device_id_type=pl.DeviceIdType.MESH)

    def arrived(ref, recv):
        remote(ref, ref, s2.at[0, 0], recv, to_x).wait_recv()

    def left(ref, send):
        remote(ref, ref, send, r1.at[0, 0], to_x).wait_send()

    def fetch(i):
        if i < 0:
            src = test.reshape(256, 4096)
        else:
            src = train.reshape(1024, 4096).at[pl.ds(i * 256, 256)]
        return pltpu.make_async_copy(src, stage.at[(i + 1) % 2], local.at[(i + 1) % 2])

    fetch(-1).start()
    fetch(0).start()
    barrier = pltpu.get_barrier_semaphore()
    for device in [to_x, to_up, to_down, to_s] + [to_lay[k] for k in others]:
        pl.semaphore_signal(barrier, inc=1, device_id=device, device_id_type=pl.DeviceIdType.MESH)

    def weigh(l, j):
        r, col = iota((64, PART), 0), iota((64, PART), 1)
        e = lax.dot_general(inv_out[l], (r == (PART // 64) * j + col // 64).astype(F32), TN,
                            precision=HIGHEST, preferred_element_type=F32)
        f = jnp.dot(inv_in[l], (r == col % 64).astype(F32), precision=HIGHEST, preferred_element_type=F32)
        weight[...] = (e[:, None, :] * f[None]).astype(BF).reshape(4096, PART)

    def precondition(l, quarter, part):
        j = quarter * 2 + part
        value = jnp.dot(amat[l], weight[...], preferred_element_type=F32).astype(BF)
        g1[quarter * 2 + l, 0, :, pl.ds(pl.multiple_of(part * PART, PART), PART)] = value[:HEAD]
        cols = pl.ds(pl.multiple_of(j * PART, PART), PART)
        for i in range(ITEMS // 2):
            g2[i * 2 + l, 0, :, cols] = value[HEAD + i * ROWS : HEAD + (i + 1) * ROWS]

    def split_layers(slot, write):
        ri, ci = iota((256, 256), 0), iota((256, 256), 1)
        order = (ci == 2 * (ri % 128) + ri // 128).astype(BF)

        @pl.loop(0, 8)
        def _(i):
            cols = pl.ds(pl.multiple_of(i * 512, 512), 512)
            write(cols, jnp.dot(order, stage[slot, :, cols], preferred_element_type=F32).astype(BF))

    def write_a(cols, value):
        amat[0, :, cols] = value[:128]
        amat[1, :, cols] = value[128:]

    def split_train(t):
        slot = lax.rem(t + 1, 2)

        def write_b(cols, value):
            rows = pl.ds(pl.multiple_of(t * 128, 128), 128)
            bmat[0, rows, cols] = value[:128]
            bmat[1, rows, cols] = value[128:]

        pltpu.make_async_copy(train.reshape(1024, 4096).at[pl.ds(0, 256)], stage.at[slot], local.at[slot]).wait()
        split_layers(slot, write_b)

        @pl.when(t < 2)
        def _():
            start = pl.multiple_of((t + 2) * 256, 256)
            pltpu.make_async_copy(train.reshape(1024, 4096).at[pl.ds(start, 256)], stage.at[slot],
                                  local.at[slot]).start()

    def prepare(p):
        l, quarter = lax.rem(p, 2), p // 2

        @pl.loop(0, 2)
        def _(part):
            weigh(l, quarter * 2 + part)
            precondition(l, quarter, part)

    half1 = [pl.ds(h * HEAD // 2, HEAD // 2) for h in (0, 1)]
    rows1, near1, far1 = pl.ds(0, HEAD), pl.ds(0, CUT1), pl.ds(CUT1, 1024 - CUT1)

    def own1(p):
        ref = g1.at[p, 0]
        remote(ref, g1.at[p, 2], s2.at[lax.rem(p, RING), 1], r1.at[p, 1], to_up).start()
        remote(ref, g1.at[p, 3], s2.at[lax.rem(p, RING), 2], r1.at[p, 2], to_down).start()
        remote(ref, g1.at[p, 1], s2.at[lax.rem(p, RING), 0], r1.at[p, 0], to_x).start()

    def first1(p):
        for h, device in ((0, to_up), (1, to_down)):
            arrived(g1.at[p, 2 + h], r1.at[p, 1 + h])
            remote(g1.at[p, 2 + h, half1[h]], g1.at[p, 6, half1[h]], s2.at[lax.rem(p, RING), 5 + h], r1h.at[p, 0, h], device).start()
            remote(g1.at[p, 2 + h, rows1, far1], g1.at[p, 4 + h, rows1, far1], s2.at[lax.rem(p, RING), 11 + h], r1c.at[p, h],
                   to_x).start()
        arrived(g1.at[p, 1], r1.at[p, 0])
        for h, device in ((0, to_up), (1, to_down)):
            remote(g1.at[p, 1, rows1, near1], g1.at[p, 4 + h, rows1, near1], s2.at[lax.rem(p, RING), 3 + h], r1.at[p, 3 + h],
                   device).start()
        remote(g1.at[p, pl.ds(0, 4)], g1.at[p, pl.ds(8, 4)], s2.at[lax.rem(p, RING), 7], r1s.at[p, 0], to_s).start()

    def second1(p):
        for h in (0, 1):
            arrived(g1.at[p, 6, half1[h]], r1h.at[p, 0, h])
            remote(g1.at[p, 6, half1[h]], g1.at[p, 7, half1[h]], s2.at[lax.rem(p, RING), 8 + h], r1h.at[p, 1, h], to_x).start()
        for h in (0, 1):
            arrived(g1.at[p, 4 + h, rows1, near1], r1.at[p, 3 + h])
            arrived(g1.at[p, 4 + h, rows1, far1], r1c.at[p, h])

    def third1(p):
        for h in (0, 1):
            arrived(g1.at[p, 7, half1[h]], r1h.at[p, 1, h])
        remote(g1.at[p, pl.ds(4, 4)], g1.at[p, pl.ds(12, 4)], s2.at[lax.rem(p, RING), 10], r1s.at[p, 1], to_s).start()

    def drain1(p):
        for k in (0, 1, 2):
            left(g1.at[p, 0], s2.at[lax.rem(p, RING), k])
        for k in (3, 4):
            left(g1.at[p, 0, rows1, near1], s2.at[lax.rem(p, RING), k])
        for k in (11, 12):
            left(g1.at[p, 0, rows1, far1], s2.at[lax.rem(p, RING), k])
        for k in (5, 6, 8, 9):
            left(g1.at[p, 0, half1[0]], s2.at[lax.rem(p, RING), k])
        for k, group in ((7, 0), (10, 1)):
            left(g1.at[p, pl.ds(0, 4)], s2.at[lax.rem(p, RING), k])

    half2 = [pl.ds(h * 2048, 2048) for h in (0, 1)]
    rows2, near2, far2 = pl.ds(0, ROWS), pl.ds(0, CUT2), pl.ds(CUT2, 4096 - CUT2)

    def own2(i):
        ref = g2.at[i, 0]
        remote(ref, g2.at[i, 2], s2.at[lax.rem(PIECES + i, RING), 1], r2.at[i, 1], to_up).start()
        remote(ref, g2.at[i, 3], s2.at[lax.rem(PIECES + i, RING), 2], r2.at[i, 2], to_down).start()
        remote(ref, g2.at[i, 1], s2.at[lax.rem(PIECES + i, RING), 0], r2.at[i, 0], to_x).start()

    def first2(i):
        for h, device in ((0, to_up), (1, to_down)):
            arrived(g2.at[i, 2 + h], r2.at[i, 1 + h])
            remote(g2.at[i, 2 + h, rows2, half2[h]], g2.at[i, 6, rows2, half2[h]], s2.at[lax.rem(PIECES + i, RING), 5 + h], r2h.at[i, 0, h],
                   device).start()
            remote(g2.at[i, 2 + h, rows2, far2], g2.at[i, 4 + h, rows2, far2], s2.at[lax.rem(PIECES + i, RING), 12 + h], r2c.at[i, h],
                   to_x).start()
        arrived(g2.at[i, 1], r2.at[i, 0])
        for h, device in ((0, to_up), (1, to_down)):
            remote(g2.at[i, 1, rows2, near2], g2.at[i, 4 + h, rows2, near2], s2.at[lax.rem(PIECES + i, RING), 3 + h], r2.at[i, 3 + h],
                   device).start()
        remote(g2.at[i, pl.ds(0, 4)], g2.at[i, pl.ds(8, 4)], s2.at[lax.rem(PIECES + i, RING), 7], r2s.at[i, 0], to_s).start()

    def second2(i):
        for h in (0, 1):
            arrived(g2.at[i, 6, rows2, half2[h]], r2h.at[i, 0, h])
            remote(g2.at[i, 6, rows2, half2[h]], g2.at[i, 7, rows2, half2[h]], s2.at[lax.rem(PIECES + i, RING), 8 + h], r2h.at[i, 1, h],
                   to_x).start()
        for h in (0, 1):
            arrived(g2.at[i, 4 + h, rows2, near2], r2.at[i, 3 + h])
            arrived(g2.at[i, 4 + h, rows2, far2], r2c.at[i, h])
        remote(g2.at[i, pl.ds(4, 3)], g2.at[i, pl.ds(12, 3)], s2.at[lax.rem(PIECES + i, RING), 10], r2s.at[i, 1], to_s).start()

    def third2(i):
        for h in (0, 1):
            arrived(g2.at[i, 7, rows2, half2[h]], r2h.at[i, 1, h])
        remote(g2.at[i, 7], g2.at[i, 15], s2.at[lax.rem(PIECES + i, RING), 11], r2s.at[i, 2], to_s).start()

    def from_sibling(i, groups):
        for group in groups:
            ref = g2.at[i, pl.ds(8, 4)] if group == 0 else g2.at[i, pl.ds(12, 3)] if group == 1 else g2.at[i, 15]
            arrived(ref, r2s.at[i, group])

    def drain2(i):
        for k in (0, 1, 2, 11):
            left(g2.at[i, 0], s2.at[lax.rem(PIECES + i, RING), k])
        for k in (3, 4):
            left(g2.at[i, 0, rows2, near2], s2.at[lax.rem(PIECES + i, RING), k])
        for k in (12, 13):
            left(g2.at[i, 0, rows2, far2], s2.at[lax.rem(PIECES + i, RING), k])
        for k in (5, 6, 8, 9):
            left(g2.at[i, 0, rows2, half2[0]], s2.at[lax.rem(PIECES + i, RING), k])
        left(g2.at[i, pl.ds(0, 4)], s2.at[lax.rem(PIECES + i, RING), 7])
        left(g2.at[i, pl.ds(4, 3)], s2.at[lax.rem(PIECES + i, RING), 10])

    def keep(q, slots, scores):
        for n, (p, k) in enumerate(slots):
            dx, dz = SLOTS[k]
            sx, sz = (1 - xh if dx else xh), lax.rem(z + dz, 4)
            row = pl.multiple_of(lax.rem(sz, 2) * 32 + (1 - c if p else c) * 16, 16)
            cs[lax.rem(q, 4), sx * 2 + sz // 2, pl.ds(row, 16), :] = scores[n * 16 : n * 16 + 16].astype(BF)

    every = [(p, k) for p in range(2) for k in range(8)]
    early = [(p, k) for p in range(2) for k in range(4)]
    late = [(p, k) for p in range(2) for k in range(4, 8)]

    def to_y(q):
        for d in (1, 2, 3):
            remote(cs.at[lax.rem(q, 4), lax.rem(y + d, 4)], yr.at[q, d - 1], ysend.at[lax.rem(q, 4), d - 1], ysem.at[q, d - 1],
                   to_lay[d, 0]).start()

    def over_y(q):
        total = cs[lax.rem(q, 4), y].astype(F32)
        for d in range(3):
            arrived(yr.at[q, d], ysem.at[q, d])
            left(yr.at[q, d], ysend.at[lax.rem(q, 4), d])
            total += yr[q, d].astype(F32)
        ysum[lax.rem(q, 4)] = total.reshape(2, 32, 512)
        xs[lax.rem(q, 4)] = ysum[lax.rem(q, 4), 1 - xl].astype(BF)
        remote(xs.at[lax.rem(q, 4)], xr.at[q], xsend.at[lax.rem(q, 4)], xsem.at[q], to_lay[0, 1]).start()

    def finish(q, total):
        for k in range(2):
            out[pl.ds(pl.multiple_of(k * 128 + q * 16, 16), 16), :] = total[k * 16 : k * 16 + 16]

    def over_x(q):
        arrived(xr.at[q], xsem.at[q])
        left(xr.at[q], xsend.at[lax.rem(q, 4)])
        finish(q, ysum[lax.rem(q, 4), xl] + xr[q].astype(F32))

    def main_head(q):
        rows = pl.ds(pl.multiple_of(q * 16, 16), 16)
        acc[1] = jnp.zeros((256, 512), F32)

        @pl.loop(0, PIECES // 2)
        def _(j):
            cols = pl.ds(pl.multiple_of(j * 1024, 1024), 1024)
            for l in (0, 1):
                lhs = g1[j * 2 + l, :, rows, :].reshape(256, 1024)
                acc[1] += lax.dot_general(lhs, bmat[l, :, cols], NT, preferred_element_type=F32)

        keep(q, every, acc[1])
        to_y(q)

    def product(l, lhs):
        return lax.dot_general(lhs, bmat[l], NT, preferred_element_type=F32)

    def main_item(n):
        l = lax.rem(n, 2)
        acc[0] = jnp.where(l == 0, jnp.zeros((256, 512), F32), acc[0]) + product(l, g2[n].reshape(256, 4096))

        @pl.when(l == 1)
        def _():
            q = HEAD // 16 + n // 2
            keep(q, every, acc[0])
            to_y(q)

    fetch(-1).wait()
    split_layers(0, write_a)
    fetch(1).start()
    prepare(0)
    pl.semaphore_wait(barrier, 11)

    end1, end2 = PIECES, PIECES + ITEMS

    @pl.loop(0, end2 + 3)
    def _(t):
        def during(start, stop, do, odd=None):
            on = (t >= start) & (t < stop)
            if odd is not None:
                on = on & (lax.rem(t, 2) == odd)
            pl.when(on)(do)

        def head_from_sibling():
            @pl.loop(0, PIECES)
            def _(p):
                for group in (0, 1):
                    arrived(g1.at[p, pl.ds(8 + 4 * group, 4)], r1s.at[p, group])


        during(RING, end1 + RING, lambda: drain1(t - RING))
        during(end1 + RING, end2 + RING, lambda: drain2(t - end1 - RING))
        during(0, end1, lambda: own1(t))
        during(end1, end2, lambda: own2(t - end1))
        during(1, end1 + 1, lambda: first1(t - 1))
        during(end1 + 1, end2 + 1, lambda: first2(t - end1 - 1))
        during(2, end1 + 2, lambda: second1(t - 2))
        during(end1 + 2, end2 + 2, lambda: second2(t - end1 - 2))
        during(0, end1 - 1, lambda: prepare(t + 1))
        during(0, end1, lambda: split_train(t // 2), 1)

        def item():
            from_sibling(t - end1 - 4, (0, 1, 2))
            main_item(t - end1 - 4)

        first_main = end1 + 3
        heads = HEAD // 16
        during(first_main, first_main + 1, head_from_sibling)
        during(first_main, first_main + heads, lambda: main_head(t - first_main))
        during(end1 + 4, end2 + 3, item)
        during(first_main + 1, first_main + 1 + heads, lambda: over_y(t - first_main - 1))
        during(end1 + 6, end2 + 3, lambda: over_y(heads + (t - end1 - 6) // 2), end1 % 2)
        during(first_main + 2, first_main + 2 + heads, lambda: over_x(t - first_main - 2))
        during(end1 + 7, end2 + 3, lambda: over_x(heads + (t - end1 - 7) // 2), 1 - end1 % 2)
        during(3, end1 + 3, lambda: third1(t - 3))
        during(end1 + 3, end2 + 2, lambda: third2(t - end1 - 3))

    i, q = ITEMS - 1, QUEUE - 1

    def last(k, slots):
        lhs = jnp.concatenate([g2[i, p + k : p + k + 4].reshape(64, 4096) for p in (0, 8)], axis=0)
        done = jnp.concatenate([acc[0, (p + k) * 16 : (p + k) * 16 + 64] for p in (0, 8)], axis=0)
        keep(q, slots, done + product(1, lhs))

    from_sibling(i, (0,))
    last(0, early)
    third2(i)

    from_sibling(i, (1, 2))
    last(4, late)
    mine = pl.ds(pl.multiple_of(xl * 32, 32), 32)
    yours = pl.ds(pl.multiple_of(32 - xl * 32, 32), 32)
    for n, (d, f) in enumerate(others):
        remote(cs.at[q % 4, lax.rem(y + d, 4), yours if f else mine], zr.at[n], zsend.at[n], zsem.at[n],
               to_lay[d, f]).start()
    for n in range(end2 + 3 - RING, end2):
        drain2(n - end1)
    total = cs[q % 4, y, mine, :].astype(F32)
    for n in range(len(others)):
        arrived(zr.at[n], zsem.at[n])
        total += zr[n].astype(F32)
    finish(q, total)
    over_x(q - 1)
    for n in range(len(others)):
        left(zr.at[n], zsend.at[n])


def body(train, test, inv_out, inv_in):
    vmem, hbm = pl.BlockSpec(memory_space=pltpu.VMEM), pl.BlockSpec(memory_space=pl.ANY)
    dma = pltpu.SemaphoreType.DMA
    return pl.pallas_call(
        kernel,
        out_shape=jax.ShapeDtypeStruct((256, 512), F32),
        in_specs=[hbm, hbm, vmem, vmem],
        out_specs=vmem,
        scratch_shapes=[
            pltpu.VMEM((PIECES, 16, HEAD, 1024), BF),
            pltpu.VMEM((ITEMS, 16, ROWS, 4096), BF),
            pltpu.VMEM((2, 512, 4096), BF),
            pltpu.VMEM((2, 256, 4096), BF),
            pltpu.VMEM((2, 128, 4096), BF),
            pltpu.VMEM((4096, PART), BF),
            pltpu.VMEM((4, 4, 64, 512), BF),
            pltpu.VMEM((QUEUE - 1, 3, 64, 512), BF),
            pltpu.VMEM((4, 32, 512), BF),
            pltpu.VMEM((QUEUE - 1, 32, 512), BF),
            pltpu.VMEM((4, 2, 32, 512), F32),
            pltpu.VMEM((7, 32, 512), BF),
            pltpu.VMEM((2, 256, 512), F32),
            dma((PIECES, 5)),
            dma((PIECES, 2, 2)),
            dma((PIECES, 2)),
            dma((PIECES, 2)),
            dma((ITEMS, 5)),
            dma((ITEMS, 2, 2)),
            dma((ITEMS, 2)),
            dma((ITEMS, 3)),
            dma((RING, 14)),
            dma((QUEUE - 1, 3)),
            dma((4, 3)),
            dma((QUEUE - 1,)),
            dma((4,)),
            dma((7,)),
            dma((7,)),
            dma((2,)),
        ],
        compiler_params=pltpu.CompilerParams(
            collective_id=0, has_side_effects=True, vmem_limit_bytes=62 * 2**20
        ),
        cost_estimate=pl.CostEstimate(flops=26 * 10**9, bytes_accessed=12 * 2**20, transcendentals=0),
    )(train, test, inv_out, inv_in)


def solution(mesh):
    return jax.shard_map(
        body,
        mesh=mesh,
        in_specs=(P("ex", "lay", None), P("ex", "lay", None), P("lay", None, None), P("lay", None, None)),
        out_specs=P("lay", "ex"),
        check_vma=False,
    )
```

time: 572 us -> 145 us (0.25)
  waiting for transfers between devices: 459 us -> 0 us
  Pallas kernels: 0 us -> 143 us
  matrix products: 46.3 us -> 0 us
  local copies, waits for them, and re-layouts: 31.4 us -> 1.87 us
  starting transfers between devices: 19.2 us -> 0 us
  between operations: 13.5 us -> 0.01 us
    ppermute x15 -> x0, waiting for transfers between devices: 383 us -> none  [shifted(): return lax.ppermute(value, axis, pairs)]
    pallas_call x0 -> x1, Pallas kernels: none -> 143 us  [body(): pl.pallas_call(kernel, out_shape=jax.ShapeDtypeStruct((256, 512), F32), i...]
    reduce_scatter x1 -> x0, waiting for transfers between devices: 75.5 us -> none  [body(): lax.psum_scatter(table.astype(jnp.bfloat16), 'lay', scatter_dimension=0,...]
    dot_general x6 -> x0, matrix products: 46.3 us -> none  [the longest x4 37.9 us: tile_scoring(): jnp.einsum('aec,jec->eaj', block_slab, training_gradient_rows, preferred_...]
    ppermute x15 -> x0, starting transfers between devices: 19.2 us -> none  [shifted(): return lax.ppermute(value, axis, pairs)]
    unnamed x12 -> x1, local copies, waits for them, and re-layouts: 20.4 us -> 1.87 us
    while x12 -> x0, local copies, waits for them, and re-layouts: 7.89 us -> none
  transfers between devices with their start and end apart: 16 -> 0, of which waited for: 16 -> 0; matrix products, arithmetic and copies ran while one was open for 2% -> 0% of each run, Pallas kernels for 0% -> 0%
where the time goes in v2:
time: 145 us
  Pallas kernels  143 us (99%)
  local copies, waits for them, and re-layouts  1.87 us (1%)
    pallas_call x1, Pallas kernels, body(): pl.pallas_call(kernel, out_shape=jax.ShapeDtypeStruct((256, 512), F32), i...  143 us

profile of v2, /device:TPU:1, one launch (start us, length us, event | category | flops | bytes accessed | tf_op | source)
XLA Modules:
  0.0 144.7 jit_solution(6388439152481570995)
XLA Ops:
  0.0 142.8 %shard_map.46 = f32[256,512]{1,0:T(8,128)} custom-call(bf16[512,2,4096]{2,1,0:T(2,128)(2,1)} %train.1, bf16[128,2,4096]{2,1,0:T(2,128)(2,1)} %test.1, f32[2,64,64]{2,1,0:T(8,128)} %inv_out.1, f32[2,64,64]{2,1,0:T(8,128)} %inv_in.1), custom_call_target="tpu_custom_call" | custom-call | flops 25999998976 | bytes 12582912 | tf_op jit(solution)/shard_map/pallas_call | solution.py:363
  142.8 1.9 %copy.6 = f32[256,512]{1,0:T(8,128)} copy(f32[256,512]{1,0:T(8,128)} %shard_map.46) | data formatting | bytes 1048576

commit v3 on v2

--- a/solution.py
+++ b/solution.py
@@ -299,7 +299,6 @@
                 for group in (0, 1):
                     arrived(g1.at[p, pl.ds(8 + 4 * group, 4)], r1s.at[p, group])
 
-
         during(RING, end1 + RING, lambda: drain1(t - RING))
         during(end1 + RING, end2 + RING, lambda: drain2(t - end1 - RING))
         during(0, end1, lambda: own1(t))
@@ -308,8 +307,6 @@
         during(end1 + 1, end2 + 1, lambda: first2(t - end1 - 1))
         during(2, end1 + 2, lambda: second1(t - 2))
         during(end1 + 2, end2 + 2, lambda: second2(t - end1 - 2))
-        during(0, end1 - 1, lambda: prepare(t + 1))
-        during(0, end1, lambda: split_train(t // 2), 1)
 
         def item():
             from_sibling(t - end1 - 4, (0, 1, 2))
@@ -325,6 +322,8 @@
         during(first_main + 2, first_main + 2 + heads, lambda: over_x(t - first_main - 2))
         during(end1 + 7, end2 + 3, lambda: over_x(heads + (t - end1 - 7) // 2), 1 - end1 % 2)
         during(3, end1 + 3, lambda: third1(t - 3))
+        during(0, end1 - 1, lambda: prepare(t + 1))
+        during(end1 - 1, end1 + 3, lambda: split_train(t - end1 + 1))
         during(end1 + 3, end2 + 2, lambda: third2(t - end1 - 3))
 
     i, q = ITEMS - 1, QUEUE - 1

time: 145 us -> 144 us (level)
  Pallas kernels: 143 us -> 141 us
where the time goes in v3:
time: 144 us; the launch traced here: 143 us
  Pallas kernels  141 us (98%)
  local copies, waits for them, and re-layouts  1.87 us (1%)
    pallas_call x1, Pallas kernels, body(): pl.pallas_call(kernel, out_shape=jax.ShapeDtypeStruct((256, 512), F32), i...  141 us

profile of v3, /device:TPU:1, one launch (start us, length us, event | category | flops | bytes accessed | tf_op | source)
XLA Modules:
  0.0 143.4 jit_solution(4235424402338099744)
XLA Ops:
  0.0 141.5 %shard_map.46 = f32[256,512]{1,0:T(8,128)} custom-call(bf16[512,2,4096]{2,1,0:T(2,128)(2,1)} %train.1, bf16[128,2,4096]{2,1,0:T(2,128)(2,1)} %test.1, f32[2,64,64]{2,1,0:T(8,128)} %inv_out.1, f32[2,64,64]{2,1,0:T(8,128)} %inv_in.1), custom_call_target="tpu_custom_call" | custom-call | flops 25999998976 | bytes 12582912 | tf_op jit(solution)/shard_map/pallas_call | solution.py:362
  141.5 1.9 %copy.6 = f32[256,512]{1,0:T(8,128)} copy(f32[256,512]{1,0:T(8,128)} %shard_map.46) | data formatting | bytes 1048576

commit v4 on v3

--- a/solution.py
+++ b/solution.py
@@ -333,9 +333,9 @@
         done = jnp.concatenate([acc[0, (p + k) * 16 : (p + k) * 16 + 64] for p in (0, 8)], axis=0)
         keep(q, slots, done + product(1, lhs))
 
+    third2(i)
     from_sibling(i, (0,))
     last(0, early)
-    third2(i)
 
     from_sibling(i, (1, 2))
     last(4, late)

time: 144 us -> 142 us (0.986)
  Pallas kernels: 141 us -> 139 us
    pallas_call x1, Pallas kernels: 141 us -> 139 us  [body(): pl.pallas_call(kernel, out_shape=jax.ShapeDtypeStruct((256, 512), F32), i...]
where the time goes in v4:
time: 142 us; the launch traced here: 141 us
  Pallas kernels  139 us (98%)
  local copies, waits for them, and re-layouts  1.87 us (1%)
    pallas_call x1, Pallas kernels, body(): pl.pallas_call(kernel, out_shape=jax.ShapeDtypeStruct((256, 512), F32), i...  139 us

profile of v4, /device:TPU:1, one launch (start us, length us, event | category | flops | bytes accessed | tf_op | source)
XLA Modules:
  0.0 141.2 jit_solution(9294338248366075356)
XLA Ops:
  0.0 139.4 %shard_map.46 = f32[256,512]{1,0:T(8,128)} custom-call(bf16[512,2,4096]{2,1,0:T(2,128)(2,1)} %train.1, bf16[128,2,4096]{2,1,0:T(2,128)(2,1)} %test.1, f32[2,64,64]{2,1,0:T(8,128)} %inv_out.1, f32[2,64,64]{2,1,0:T(8,128)} %inv_in.1), custom_call_target="tpu_custom_call" | custom-call | flops 25999998976 | bytes 12582912 | tf_op jit(solution)/shard_map/pallas_call | solution.py:362
  139.4 1.9 %copy.6 = f32[256,512]{1,0:T(8,128)} copy(f32[256,512]{1,0:T(8,128)} %shard_map.46) | data formatting | bytes 1048576

commit v5 on v4

--- a/solution.py
+++ b/solution.py
@@ -17,7 +17,7 @@
 ITEMS = 8
 QUEUE = 8
 PART = 512
-CUT1, CUT2 = 896, 3584
+CUT1, CUT2 = 896, 3840
 RING = 5
 
 
@@ -25,7 +25,7 @@
     return lax.broadcasted_iota(jnp.int32, shape, dim)
 
 
-def kernel(train, test, inv_out, inv_in, out, g1, g2, bmat, stage, amat, weight, cs, yr, xs, xr, ysum, zr, acc,
+def kernel(train, test, inv_out, inv_in, result, out, osem, g1, g2, bmat, stage, amat, weight, cs, yr, xs, xr, ysum, zr, acc,
            r1, r1h, r1c, r1s, r2, r2h, r2c, r2s, s2, ysem, ysend, xsem, xsend, zsem, zsend, local):
     ex, lay = lax.axis_index("ex"), lax.axis_index("lay")
     xh, z, c = ex // 8, (ex // 2) % 4, ex % 2
@@ -120,9 +120,9 @@
 
     def own1(p):
         ref = g1.at[p, 0]
+        remote(ref, g1.at[p, 1], s2.at[lax.rem(p, RING), 0], r1.at[p, 0], to_x).start()
         remote(ref, g1.at[p, 2], s2.at[lax.rem(p, RING), 1], r1.at[p, 1], to_up).start()
         remote(ref, g1.at[p, 3], s2.at[lax.rem(p, RING), 2], r1.at[p, 2], to_down).start()
-        remote(ref, g1.at[p, 1], s2.at[lax.rem(p, RING), 0], r1.at[p, 0], to_x).start()
 
     def first1(p):
         for h, device in ((0, to_up), (1, to_down)):
@@ -166,9 +166,9 @@
 
     def own2(i):
         ref = g2.at[i, 0]
+        remote(ref, g2.at[i, 1], s2.at[lax.rem(PIECES + i, RING), 0], r2.at[i, 0], to_x).start()
         remote(ref, g2.at[i, 2], s2.at[lax.rem(PIECES + i, RING), 1], r2.at[i, 1], to_up).start()
         remote(ref, g2.at[i, 3], s2.at[lax.rem(PIECES + i, RING), 2], r2.at[i, 2], to_down).start()
-        remote(ref, g2.at[i, 1], s2.at[lax.rem(PIECES + i, RING), 0], r2.at[i, 0], to_x).start()
 
     def first2(i):
         for h, device in ((0, to_up), (1, to_down)):
@@ -318,7 +318,7 @@
         during(first_main, first_main + heads, lambda: main_head(t - first_main))
         during(end1 + 4, end2 + 3, item)
         during(first_main + 1, first_main + 1 + heads, lambda: over_y(t - first_main - 1))
-        during(end1 + 6, end2 + 3, lambda: over_y(heads + (t - end1 - 6) // 2), end1 % 2)
+        during(end1 + 6, end2 + 2, lambda: over_y(heads + (t - end1 - 6) // 2), end1 % 2)
         during(first_main + 2, first_main + 2 + heads, lambda: over_x(t - first_main - 2))
         during(end1 + 7, end2 + 3, lambda: over_x(heads + (t - end1 - 7) // 2), 1 - end1 % 2)
         during(3, end1 + 3, lambda: third1(t - 3))
@@ -334,6 +334,13 @@
         keep(q, slots, done + product(1, lhs))
 
     third2(i)
+
+    def leave(k, first, rows, sem):
+        part = pl.ds(k * 128 + first, rows)
+        return pltpu.make_async_copy(out.at[part], result.at[part], osem.at[sem])
+
+    for k in range(2):
+        leave(k, 0, 96, k).start()
     from_sibling(i, (0,))
     last(0, early)
 
@@ -346,14 +353,20 @@
                to_lay[d, f]).start()
     for n in range(end2 + 3 - RING, end2):
         drain2(n - end1)
+    over_y(q - 1)
     total = cs[q % 4, y, mine, :].astype(F32)
     for n in range(len(others)):
         arrived(zr.at[n], zsem.at[n])
         total += zr[n].astype(F32)
     finish(q, total)
     over_x(q - 1)
+    for k in range(2):
+        leave(k, 96, 32, 2 + k).start()
     for n in range(len(others)):
         left(zr.at[n], zsend.at[n])
+    for k in range(2):
+        leave(k, 0, 96, k).wait()
+        leave(k, 96, 32, 2 + k).wait()
 
 
 def body(train, test, inv_out, inv_in):
@@ -363,8 +376,10 @@
         kernel,
         out_shape=jax.ShapeDtypeStruct((256, 512), F32),
         in_specs=[hbm, hbm, vmem, vmem],
-        out_specs=vmem,
+        out_specs=hbm,
         scratch_shapes=[
+            pltpu.VMEM((256, 512), F32),
+            dma((4,)),
             pltpu.VMEM((PIECES, 16, HEAD, 1024), BF),
             pltpu.VMEM((ITEMS, 16, ROWS, 4096), BF),
             pltpu.VMEM((2, 512, 4096), BF),

time: 142 us -> 141 us (level)
  no operation moved by 1% of the time
where the time goes in v5:
time: 141 us
  Pallas kernels  139 us (99%)
  local copies, waits for them, and re-layouts  1.87 us (1%)
    pallas_call x1, Pallas kernels, body(): pl.pallas_call(kernel, out_shape=jax.ShapeDtypeStruct((256, 512), F32), i...  139 us

profile of v5, /device:TPU:1, one launch (start us, length us, event | category | flops | bytes accessed | tf_op | source)
XLA Modules:
  0.0 140.6 jit_solution(3956038071448861214)
XLA Ops:
  0.0 138.7 %shard_map.46 = f32[256,512]{1,0:T(8,128)} custom-call(bf16[512,2,4096]{2,1,0:T(2,128)(2,1)} %train.1, bf16[128,2,4096]{2,1,0:T(2,128)(2,1)} %test.1, f32[2,64,64]{2,1,0:T(8,128)} %inv_out.1, f32[2,64,64]{2,1,0:T(8,128)} %inv_in.1), custom_call_target="tpu_custom_call" | custom-call | flops 25999998976 | bytes 12582912 | tf_op jit(solution)/shard_map/pallas_call | solution.py:375
  138.7 1.9 %copy.6 = f32[256,512]{1,0:T(8,128)} copy(f32[256,512]{1,0:T(8,128)} %shard_map.46) | data formatting | bytes 1048576
